TPU v7x, 256 devices: a whole 4x4x8 slice. The times are simulated.
256 devices in a mesh: member: 8 (over x, core), tx: 4 (over y), ty: 8 (over z).
Axes of the slice: x: 4, y: 4, z: 8, core: 2. Of those that a mesh axis runs over, the one named last changes fastest.
Arguments:
- state: float32 [4096, 256, 128], P(('member', 'tx'), 'ty'), parts along dimension 0, may hold values from -6 to 6
- courant: bfloat16 [4096, 256, 128], P(('member', 'tx'), 'ty'), parts along dimension 0, may hold values from -0.3984375 to 0.3984375
- diffusion: float32 [4096, 256], P(('member', 'tx'), 'ty'), parts along dimension 0, may hold values from 0.02 to 0.2
- conv_mask: int32 [4096, 256], P(('member', 'tx'), 'ty'), parts along dimension 0, may hold values from 0 to 1, as said below
- w_in: bfloat16 [128, 1024], replicated, may hold values from -0.5 to 0.5
- w_hidden: bfloat16 [3, 1024, 1024], replicated, may hold values from -0.1875 to 0.1875
- w_out: bfloat16 [1024, 128], replicated, may hold values from -0.1875 to 0.1875
Outputs:
- state_out: float32 [4096, 256, 128], P(('member', 'tx'), 'ty'), parts along dimension 0
There are 8 independent parts, one for each index of `member`. A program takes and returns all parts, laid end to end along the dimension named above; an argument that names none is the same for every part. Nothing has to cross between parts.
Inputs may be any that keep to these rules, and one draw needn't show every extreme that they name: `conv_mask`: A tile is one device's 128 x 32 columns. A tile's used blocks are ceil(its flagged columns / 32); at most 64, reached by some tile; over a member's tiles they sum to exactly 1056.
All inputs are finite; a program needn't handle non-finite values.
Results may differ from a plain program's by a relative error of at most 0.00033.
Values may be sent and summed in bfloat16 or wider, within the bound.
No kernel may reach another device: no remote copies, remote signals or barrier semaphores. Data moves between devices by JAX's collectives and lax.ppermute only.
A program may use at most 64 MiB of HBM per device.

v0:
```python
import functools

import jax
import jax.numpy as jnp
from jax import lax
from jax.experimental import pallas as pl
from jax.experimental.pallas import tpu as pltpu
from jax.sharding import PartitionSpec as P

LON, LAT, CH, HID = 128, 32, 128, 1024
COLS = LON * LAT
TILE = 512
CAP = 2048
ROWS = CAP + TILE
PGRP = 256
UGRP = 128
EDGE = 384
EARLY = 6
UNIT = 256
BF, F32, I32 = jnp.bfloat16, jnp.float32, jnp.int32


def iota(shape, dim):
    return lax.broadcasted_iota(I32, shape, dim)


def one_hot(hit):
    return jnp.where(hit, F32(1.0), F32(0.0)).astype(BF)


def mm(a, b):
    return jnp.dot(a, b, preferred_element_type=F32)


def silu(v):
    half = 0.5 * v
    return (half + half * jnp.tanh(half)).astype(BF)


def closure_tile(x, w_in, w_hid, w_out, ha, hb, beside=()):
    step = 256
    beside = list(beside)
    ha, hb = ha.at[: x.shape[0]], hb.at[: x.shape[0]]

    def layer(src, weight, dst, side):
        for n in range(0, HID, step):
            dst[:, n : n + step] = silu(mm(src, weight(n)))
            if side and n in (0, 512) and beside:
                beside.pop(0)()

    layer(x, lambda n: w_in[:, n : n + step], ha, False)
    layer(ha[...], lambda n: w_hid[0, :, n : n + step], hb, True)
    layer(hb[...], lambda n: w_hid[1, :, n : n + step], ha, True)
    layer(ha[...], lambda n: w_hid[2, :, n : n + step], hb, True)
    return mm(hb[...], w_out[...]).astype(BF)


def append(packed, rows, aligned):
    n = rows.shape[0]
    head = packed[pl.ds(aligned, 16), :].astype(F32) + rows[:16]
    packed[pl.ds(aligned, 16), :] = head.astype(BF)
    packed[pl.ds(pl.multiple_of(aligned + 16, 16), n - 16), :] = rows[16:].astype(BF)


def align16(x):
    return pl.multiple_of((x // 16) * 16, 16)


def first_kernel(
    state_h, courant_h, diff_h, mask_h, win_h, whid_h, wout_h,
    adv, packed, tend, rank_t, rank_e, scal, coef, w_in, w_hid, w_out, lon_lo, lon_hi, lat_lo, lat_hi,
    st, cou, feat, dif, dif_n, msk, rank_n, rank_r, ha, hb, scal_v, sem, sem_s,
):
    quarter = COLS // 4

    def in_copies(k):
        return (
            pltpu.make_async_copy(state_h.at[pl.ds(k * quarter, quarter)], st.at[pl.ds(k * quarter + LAT, quarter)], sem.at[k]),
            pltpu.make_async_copy(courant_h.at[pl.ds(k * quarter, quarter)], cou.at[pl.ds(k * quarter, quarter)], sem.at[4 + k]),
        )

    mask_copy = pltpu.make_async_copy(mask_h, msk, sem.at[8])
    diff_copy = pltpu.make_async_copy(diff_h, dif, sem.at[9])
    w_copies = (
        pltpu.make_async_copy(win_h, w_in, sem.at[10]),
        pltpu.make_async_copy(whid_h, w_hid, sem.at[11]),
        pltpu.make_async_copy(wout_h, w_out, sem.at[12]),
    )
    mask_copy.start()
    diff_copy.start()
    for k in range(4):
        for c in in_copies(k):
            c.start()
    for c in w_copies:
        c.start()
    packed[...] = jnp.zeros_like(packed)
    st[0:LAT, :] = jnp.zeros((LAT, CH), F32)
    st[COLS + LAT : COLS + 2 * LAT, :] = jnp.zeros((LAT, CH), F32)

    def wait_quarter(k):
        for c in in_copies(k):
            c.wait()

    mask_copy.wait()
    diff_copy.wait()
    wait_quarter(0)
    wait_quarter(1)
    dif_1 = dif[...].astype(BF).astype(F32)
    dif_2 = (dif[...] - dif_1).astype(BF).astype(F32)
    dif_3 = dif[...] - dif_1 - dif_2
    dif_n[...] = jnp.transpose(jnp.concatenate([dif_1, dif_2, dif_3, jnp.zeros((LAT, LON), F32)], axis=0))

    lat_of = iota((LAT, CH), 0)
    low = iota((LAT, CH), 1) < 64
    own_lat = (iota((LAT, CH), 1) & 31) == lat_of
    ones = jnp.ones((CH, CH), BF)

    def stencil(i):
        spread = [jnp.where(own_lat, dif_n[pl.ds(i * 16 + j, 1), :], F32(0.0)) for j in range(16)]
        d_all = mm(jnp.concatenate(spread, axis=0).astype(BF), ones)
        for j in range(16):
            r = pl.multiple_of(i * 2 * PGRP + j * LAT, LAT)
            center = st[pl.ds(r + LAT, LAT), :]
            east = st[pl.ds(r + 2 * LAT, LAT), :]
            west = st[pl.ds(r, LAT), :]
            north = jnp.where(lat_of == LAT - 1, F32(0.0), st[pl.ds(r + LAT + 1, LAT), :])
            south = jnp.where(lat_of == 0, F32(0.0), st[pl.ds(r + LAT - 1, LAT), :])
            wind = 0.5 * cou[pl.ds(r, LAT), :].astype(F32)
            turned = pltpu.roll(wind, 64, 1)
            along_lon = jnp.where(low, wind, turned)
            along_lat = jnp.where(low, turned, wind)
            d = d_all[j * LAT : (j + 1) * LAT]
            laplace = east + west + north + south - 4.0 * center
            new = center - along_lon * (east - west) - along_lat * (north - south) + d * laplace
            adv[pl.ds(r, LAT), :] = new
            feat[pl.ds(r, LAT), :] = new.astype(BF)
            coef[pl.ds(i * 16 + j, 1), :] = (d - along_lat)[LAT - 1 :]
            coef[pl.ds(LON + i * 16 + j, 1), :] = (d + along_lat)[:1]
            if isinstance(i, int) and i == 0 and j == 0:
                coef[2 * LON : 2 * LON + LAT, :] = d + along_lon
            if isinstance(i, int) and i == 7 and j == 15:
                coef[2 * LON + LAT : 2 * LON + 2 * LAT, :] = d - along_lon

    lat, lon = iota((LAT, LON), 0), iota((LAT, LON), 1)
    flags = msk[...]
    inner = (lon > 0) & (lon < LON - 1) & (lat > 0) & (lat < LAT - 1) & (flags == 1)
    inner_b = one_hot(inner)
    in_row = mm(one_hot(iota((LAT, LAT), 1) < iota((LAT, LAT), 0)), inner_b)
    per_lon = mm(jnp.ones((LAT, LAT), BF), inner_b).astype(BF)
    row_start = mm(per_lon, one_hot(iota((LON, LON), 0) < iota((LON, LON), 1)))
    rank = jnp.where(inner, in_row + row_start, F32(-4096.0))
    rank_t[...] = rank.astype(I32)
    starts = row_start[:1]
    flags_f = flags.astype(F32)
    lane = iota((1, LON), 1)
    ends = (lane == 0) | (lane == LON - 1)
    both = jnp.concatenate([rank, flags_f, jnp.zeros((LON - 2 * LAT, LON), F32)], axis=0)
    rank_n[...] = jnp.transpose(both)
    edge_row = jnp.concatenate(
        [
            rank_n[0:1, LAT : 2 * LAT],
            rank_n[LON - 1 :, LAT : 2 * LAT],
            jnp.zeros((1, 64), F32),
            jnp.where(ends, F32(0.0), flags_f[:1]),
            jnp.where(ends, F32(0.0), flags_f[LAT - 1 :]),
        ],
        axis=1,
    )
    edge_n = jnp.broadcast_to(jnp.sum(edge_row, axis=1, keepdims=True), (1, LON))
    stencil(0)
    scal_v[...] = jnp.where(iota((8, LON), 0) == 0, starts, edge_n).astype(I32)
    scal_copy = pltpu.make_async_copy(scal_v, scal, sem_s)
    scal_copy.start()
    rank_r[...] = jnp.concatenate(
        [rank_n[pl.ds(j, COLS // PGRP, stride=PGRP // LAT), :LAT] for j in range(PGRP // LAT)], axis=1
    ).astype(I32)
    edge_b = jnp.broadcast_to(edge_row, (16, EDGE)).astype(BF)
    edge_rank = mm(edge_b, one_hot(iota((EDGE, EDGE), 0) < iota((EDGE, EDGE), 1)))[:8]
    rank_e[...] = jnp.where(edge_row == 1.0, edge_rank + starts[:, LON - 1 :], F32(-4096.0)).astype(I32)
    def pack(i):
        todo = []
        for k in range(2):
            g = i * 2 + k
            aligned = align16(scal[0, g * 8])
            hits = iota((PGRP + 16, PGRP), 0) == rank_r[pl.ds(g, 1), :] - aligned
            todo.append((aligned, mm(one_hot(hits), feat[pl.ds(pl.multiple_of(g * PGRP, PGRP), PGRP), :])))
        for aligned, rows in todo:
            append(packed, rows, aligned)

    scal_copy.wait()

    def both_steps(i, carry):
        @pl.when((lax.rem(i, 2) == 1) & (i > 1))
        def _():
            wait_quarter(lax.div(i, 2) + 1)

        stencil(i)
        pack(i - 1)
        return carry

    lax.fori_loop(1, 7, both_steps, 0)
    stencil(7)
    pack(6)
    pack(7)
    lon_lo[...] = st[LAT : 2 * LAT, :]
    lon_hi[...] = st[COLS : COLS + LAT, :]
    lat_lo[...] = st[pl.ds(LAT, LON, stride=LAT), :]
    lat_hi[...] = st[pl.ds(2 * LAT - 1, LON, stride=LAT), :]
    for c in w_copies:
        c.wait()

    before, _, _ = plan(scal)
    weights, hidden = (w_in, w_hid, w_out), (ha, hb)

    @pl.when(before == 2)
    def _():
        tend[...] = closure_tile(packed[:TILE, :], *weights, *hidden)

    @pl.when(before == 1)
    def _():
        tend[:UNIT, :] = closure_tile(packed[:UNIT, :], *weights, *hidden)


def closure_units(packed, tend, weights, hidden, first, end):
    def rows(unit, size):
        part = pl.ds(pl.multiple_of(unit * UNIT, UNIT), size)
        tend[part, :] = closure_tile(packed[part, :], *weights, *hidden)

    odd = lax.rem(end - first, 2)

    @pl.when(odd == 1)
    def _():
        rows(first, UNIT)

    def tile(t, carry):
        rows(first + odd + 2 * t, TILE)
        return carry

    lax.fori_loop(0, lax.div(end - first, 2), tile, 0)


def plan(scal):
    inner_n = scal[0, LON - 1]
    count = inner_n + scal[1, 0]
    total = lax.div(count + UNIT - 1, UNIT)
    before = jnp.where(count >= 1536, 2, jnp.where(count >= 1280, 1, 0))
    inner = lax.div(inner_n, UNIT)
    less = (inner > before) & (lax.rem(inner - before, 2) == 1) & (total - inner < 2)
    return before, jnp.where(less, inner - 1, inner), total


def middle_kernel(packed, tend_f, scal, w_in, w_hid, w_out, tend, ha, hb):
    tend[...] = jnp.zeros_like(tend)
    before, inner, _ = plan(scal)

    @pl.when(before >= 1)
    def _():
        tend[:UNIT, :] = tend_f[:UNIT, :]

    @pl.when(before == 2)
    def _():
        tend[UNIT:TILE, :] = tend_f[UNIT:, :]

    closure_units(packed, tend, (w_in, w_hid, w_out), (ha, hb), before, inner)


def last_kernel(
    west, east, south, north, adv_i, packed_i, tend_i, rank_t, rank_e, scal, coef, w_in, w_hid, w_out,
    out_h, adv, packed, tend, ha, hb, sem,
):
    adv[0:LAT, :] += west[...] * coef[2 * LON : 2 * LON + LAT, :]
    adv[COLS - LAT :, :] += east[...] * coef[2 * LON + LAT :, :]
    low, high = pl.ds(0, LON, stride=LAT), pl.ds(LAT - 1, LON, stride=LAT)
    place = lax.axis_index("ty")
    north_rim = jnp.where(place == lax.axis_size("ty") - 1, F32(0.0), north[...])
    south_rim = jnp.where(place == 0, F32(0.0), south[...])
    adv[high, :] = adv[high, :] + north_rim * coef[:LON, :]
    adv[low, :] = adv[low, :] + south_rim * coef[LON : 2 * LON, :]
    edge = jnp.concatenate(
        [adv[0:LAT, :], adv[COLS - LAT :, :], jnp.zeros((64, CH), F32), adv[low, :], adv[high, :]], axis=0
    ).astype(BF)
    inner_n = scal[0, LON - 1]
    aligned_e = align16(inner_n)
    hits = iota((320 + 16, EDGE), 0) == rank_e[:1, :] - aligned_e
    append(packed, mm(one_hot(hits), edge), aligned_e)

    def unpacked(q):
        turned = pltpu.roll(rank_t[...], lax.rem(LON - q * 16, LON), 1)
        parts = []
        for i in range(4):
            aligned = align16(scal[0, q * 16 + 4 * i])
            cols = [jnp.broadcast_to(turned[:, 4 * i + j : 4 * i + j + 1], (LAT, 256)) for j in range(4)]
            hit = one_hot(jnp.concatenate(cols, axis=0) == iota((UGRP, 256), 1) + aligned)
            parts.append(mm(hit, tend[pl.ds(aligned, 256), :]))
        r = pl.multiple_of(q * 4 * UGRP, 4 * UGRP)
        adv[pl.ds(r, 4 * UGRP), :] += jnp.concatenate(parts, axis=0)

    _, done, total = plan(scal)
    early = (total - done >= 2) & (scal[0, EARLY * 16] <= (total - 2) * UNIT)
    weights, hidden = (w_in, w_hid, w_out), (ha, hb)
    closure_units(packed, tend, weights, hidden, done, jnp.where(early, total - 2, total))

    @pl.when(early)
    def _():
        part = pl.ds(pl.multiple_of((total - 2) * UNIT, UNIT), TILE)
        beside = [functools.partial(unpacked, q) for q in range(EARLY)]
        tend[part, :] = closure_tile(packed[part, :], *weights, *hidden, beside)

    rank_col = jnp.concatenate(
        [jnp.transpose(jnp.broadcast_to(rank_e[:1, k * 128 : k * 128 + 128], (128, 128))) for k in range(3)], axis=0
    )
    picks = jnp.concatenate([rank_col - aligned_e - 128 * k for k in range(3)], axis=1) == (
        iota((EDGE, EDGE), 1) & 127
    )
    back = mm(one_hot(picks), tend[pl.ds(aligned_e, EDGE), :])
    adv[0:LAT, :] += back[0:LAT]
    adv[COLS - LAT :, :] += back[LAT : 2 * LAT]
    adv[low, :] = adv[low, :] + back[128:256]
    adv[high, :] = adv[high, :] + back[256:384]

    def out_copy(k):
        part = pl.ds(k * (COLS // 8), COLS // 8)
        return pltpu.make_async_copy(adv.at[part], out_h.at[part], sem.at[k])

    def unpack(q, carry):
        @pl.when(jnp.logical_not(early) | (q >= EARLY))
        def _():
            unpacked(q)

        out_copy(q).start()
        return carry

    lax.fori_loop(0, 8, unpack, 0)
    for k in range(8):
        out_copy(k).wait()


ANY = pl.BlockSpec(memory_space=pl.ANY)
HBM = pl.BlockSpec(memory_space=pltpu.HBM)
VM = pl.BlockSpec(memory_space=pltpu.VMEM)
SM = pl.BlockSpec(memory_space=pltpu.SMEM)


def in_hbm(x):
    return pltpu.with_memory_space_constraint(x, pltpu.HBM)


def params():
    return pltpu.CompilerParams(vmem_limit_bytes=24 << 20)


def cost(gflops):
    return pl.CostEstimate(flops=gflops * 10**9, bytes_accessed=1 << 20, transcendentals=1 << 20)


def local(state, courant, diffusion, conv_mask, w_in, w_hidden, w_out):
    n_tx, n_ty = lax.axis_size("tx"), lax.axis_size("ty")
    ring = [(i, (i + 1) % n_tx) for i in range(n_tx)]
    line = [(i, (i + 1) % n_ty) for i in range(n_ty)]
    kept = (
        ((COLS, CH), F32),
        ((ROWS, CH), BF),
        ((TILE, CH), BF),
        ((LAT, LON), I32),
        ((8, EDGE), I32),
        None,
        ((2 * LON + 2 * LAT, CH), F32),
        ((CH, HID), BF),
        ((3, HID, HID), BF),
        ((HID, CH), BF),
        ((LAT, CH), F32),
        ((LAT, CH), F32),
        ((LON, CH), F32),
        ((LON, CH), F32),
    )
    hidden = [pltpu.VMEM((TILE, HID), BF)] * 2
    held = pl.pallas_call(
        first_kernel,
        out_shape=[pltpu.VMEM(*k) if k else pltpu.SMEM((8, LON), I32) for k in kept],
        in_specs=[HBM] * 7,
        out_specs=[VM if k else SM for k in kept],
        scratch_shapes=[
            pltpu.VMEM((COLS + 2 * LAT + 8, CH), F32),
            pltpu.VMEM((COLS, CH), BF),
            pltpu.VMEM((COLS, CH), BF),
            pltpu.VMEM((LAT, LON), F32),
            pltpu.VMEM((LON, LON), F32),
            pltpu.VMEM((LAT, LON), I32),
            pltpu.VMEM((LON, LON), F32),
            pltpu.VMEM((COLS // PGRP, PGRP), I32),
            *hidden,
            pltpu.VMEM((8, LON), I32),
            pltpu.SemaphoreType.DMA((13,)),
            pltpu.SemaphoreType.DMA,
        ],
        compiler_params=params(),
        cost_estimate=cost(1),
        name="advance_pack",
    )(*map(in_hbm, (state.reshape(COLS, CH), courant.reshape(COLS, CH), diffusion.T, conv_mask.T, w_in, w_hidden, w_out)))
    adv, packed, tend_f, rank_t, rank_e, scal, coef, w_in, w_hid, w_out, lon_lo, lon_hi, lat_lo, lat_hi = held
    west = lax.ppermute(lon_hi, "tx", ring)
    east = lax.ppermute(lon_lo, "tx", [(j, i) for i, j in ring])
    south = lax.ppermute(lat_hi, "ty", line)
    north = lax.ppermute(lat_lo, "ty", [(j, i) for i, j in line])
    tend = pl.pallas_call(
        middle_kernel,
        out_shape=pltpu.VMEM((ROWS, CH), BF),
        in_specs=[VM, VM, SM, VM, VM, VM],
        out_specs=VM,
        scratch_shapes=hidden,
        compiler_params=params(),
        cost_estimate=cost(12),
        name="closure_middle",
    )(packed, tend_f, scal, w_in, w_hid, w_out)
    out, *_ = pl.pallas_call(
        last_kernel,
        out_shape=[
            jax.ShapeDtypeStruct((COLS, CH), F32),
            pltpu.VMEM((COLS, CH), F32),
            pltpu.VMEM((ROWS, CH), BF),
            pltpu.VMEM((ROWS, CH), BF),
        ],
        in_specs=[VM] * 9 + [SM] + [VM] * 4,
        out_specs=[HBM, VM, VM, VM],
        input_output_aliases={4: 1, 5: 2, 6: 3},
        scratch_shapes=[*hidden, pltpu.SemaphoreType.DMA((8,))],
        compiler_params=params(),
        cost_estimate=cost(4),
        name="closure_unpack",
    )(west, east, south, north, adv, packed, tend, rank_t, rank_e, scal, coef, w_in, w_hid, w_out)
    return out.reshape(LON, LAT, CH)


def solution(mesh):
    tile = P(("member", "tx"), "ty", None)
    flat = P(("member", "tx"), "ty")
    return jax.shard_map(
        local,
        mesh=mesh,
        in_specs=(tile, tile, flat, flat, P(), P(), P()),
        out_specs=tile,
        check_vma=False,
    )
```

profile of v0, /device:TPU:5, one launch (start us, length us, event | category | flops | bytes accessed | tf_op | source)
XLA Modules:
  0.0 35.0 jit_solution(17114236241610916017)
XLA Ops:
  0.0 8.7 %advance_pack.1 = (f32[4096,128]{1,0:T(8,128)S(1)}, bf16[2560,128]{1,0:T(8,128)(2,1)S(1)}, bf16[512,128]{1,0:T(8,128)(2,1)S(1)}, s32[32,128]{1,0:T(8,128)S(1)}, ...) custom-call(f32[4096,128]{1,0:T(8,128)} %bitcast.5, ...), custom_call_target="tpu_custom_call" | custom-call | flops 1000000000 | bytes 1048576 | tf_op jit(solution)/shard_map/advance_pack/pallas_call | solution.py:377
  8.7 0.1 collective-permute-start
  8.8 2.7 %collective-permute-start.1 = (f32[32,128]{1,0:T(8,128)S(1)}, f32[32,128]{1,0:T(8,128)S(1)}, u32[]{:S(2)}, u32[]{:S(2)}) collective-permute-start(f32[32,128]{1,0:T(8,128)S(1)} %get-tuple-element.21), channel_id=1, source_target_pairs={{8,0},{16,8},{24,16},{0,24},{9,1},{17,9},{25,17},{1,25},{10,2},{18... | collective-permute-start | bytes 49160 | tf_op jit(solution)/shard_map/ppermute | solution.py:402
  11.4 3.4 %collective-permute-start.2 = (f32[128,128]{1,0:T(8,128)S(1)}, f32[128,128]{1,0:T(8,128)S(1)}, u32[]{:S(2)}, u32[]{:S(2)}) collective-permute-start(f32[128,128]{1,0:T(8,128)S(1)} %get-tuple-element.22), channel_id=1, source_target_pairs={{0,1},{1,2},{2,3},{3,4},{4,5},{5,6},{6,7},{7,0},{8,9},{9,10},{10,1... | collective-permute-start | bytes 196616 | tf_op jit(solution)/shard_map/ppermute | solution.py:403
  14.9 3.9 %collective-permute-start.3 = (f32[128,128]{1,0:T(8,128)S(1)}, f32[128,128]{1,0:T(8,128)S(1)}, u32[]{:S(2)}, u32[]{:S(2)}) collective-permute-start(f32[128,128]{1,0:T(8,128)S(1)} %get-tuple-element.23), channel_id=1, source_target_pairs={{1,0},{2,1},{3,2},{4,3},{5,4},{6,5},{7,6},{0,7},{9,8},{10,9},{11,1... | collective-permute-start | bytes 196616 | tf_op jit(solution)/shard_map/ppermute | solution.py:404
  18.8 8.7 %closure_middle.1.tend_i = bf16[2560,128]{1,0:T(8,128)(2,1)S(1)} custom-call(bf16[2560,128]{1,0:T(8,128)(2,1)S(1)} %get-tuple-element.25.packed.packed_i, bf16[512,128]{1,0:T(8,128)(2,1)S(1)} %get-tuple-element.26.tend_f, s32[8,128]{1,0:T(8,128)S(4)} %get-tuple-element.27.scal, bf16[128,1024]{1,0:T(8,128)(2,1)S(1)} %get-tuple-element.28.w_in, ...), custom_call_target="tpu_custom_call" | custom-call | flops 12000000000 | bytes 1048576 | tf_op jit(solution)/shard_map/closure_middle/pallas_call | solution.py:405
  27.5 0.0 collective-permute-done.west
  27.5 0.0 collective-permute-done.1.east
  27.5 0.0 collective-permute-done.2.south
  27.5 0.0 collective-permute-done.3.north
  27.5 7.4 %closure_unpack.1 = (f32[4096,128]{1,0:T(8,128)}, f32[4096,128]{1,0:T(8,128)S(1)}, bf16[2560,128]{1,0:T(8,128)(2,1)S(1)}, bf16[2560,128]{1,0:T(8,128)(2,1)S(1)}) custom-call(f32[32,128]{1,0:T(8,128)S(1)} %collective-permute-done.west, f32[32,128]{1,0:T(8,128)S(1)} %collective-permute-done.1.east, ...), custom_call_target="tpu_custom_call", output_to_operand_aliasing={{1}: (4, {}), {2}: (5, {}), {3}: (6, {})} | custom-call | flops 4000000000 | bytes 1048576 | tf_op jit(solution)/shard_map/closure_unpack/pallas_call | solution.py:415
Async XLA Ops:
  8.7 18.8 %collective-permute-start = (f32[32,128]{1,0:T(8,128)S(1)}, f32[32,128]{1,0:T(8,128)S(1)}, u32[]{:S(2)}, u32[]{:S(2)}) collective-permute-start(f32[32,128]{1,0:T(8,128)S(1)} %get-tuple-element.20), channel_id=1, source_target_pairs={{0,8},{8,16},{16,24},{24,0},{1,9},{9,17},{17,25},{25,1},{2,10},{10... | collective-permute-start | bytes 49160 | tf_op jit(solution)/shard_map/ppermute | solution.py:401
  8.8 18.7 %collective-permute-start.1 = (f32[32,128]{1,0:T(8,128)S(1)}, f32[32,128]{1,0:T(8,128)S(1)}, u32[]{:S(2)}, u32[]{:S(2)}) collective-permute-start(f32[32,128]{1,0:T(8,128)S(1)} %get-tuple-element.21), channel_id=1, source_target_pairs={{8,0},{16,8},{24,16},{0,24},{9,1},{17,9},{25,17},{1,25},{10,2},{18... | collective-permute-start | bytes 49160 | tf_op jit(solution)/shard_map/ppermute | solution.py:402
  11.4 16.1 %collective-permute-start.2 = (f32[128,128]{1,0:T(8,128)S(1)}, f32[128,128]{1,0:T(8,128)S(1)}, u32[]{:S(2)}, u32[]{:S(2)}) collective-permute-start(f32[128,128]{1,0:T(8,128)S(1)} %get-tuple-element.22), channel_id=1, source_target_pairs={{0,1},{1,2},{2,3},{3,4},{4,5},{5,6},{6,7},{7,0},{8,9},{9,10},{10,1... | collective-permute-start | bytes 196616 | tf_op jit(solution)/shard_map/ppermute | solution.py:403
  14.9 12.6 %collective-permute-start.3 = (f32[128,128]{1,0:T(8,128)S(1)}, f32[128,128]{1,0:T(8,128)S(1)}, u32[]{:S(2)}, u32[]{:S(2)}) collective-permute-start(f32[128,128]{1,0:T(8,128)S(1)} %get-tuple-element.23), channel_id=1, source_target_pairs={{1,0},{2,1},{3,2},{4,3},{5,4},{6,5},{7,6},{0,7},{9,8},{10,9},{11,1... | collective-permute-start | bytes 196616 | tf_op jit(solution)/shard_map/ppermute | solution.py:404
where the time goes:
time: 35.3 us; the launch traced here: 35 us
  Pallas kernels  24.7 us (70%)
  starting transfers between devices  10.1 us (29%)
    pallas_call x1, Pallas kernels, local(): pl.pallas_call(first_kernel, out_shape=[pltpu.VMEM(*k) if k else pltpu.SM...  8.66 us
    pallas_call x1, Pallas kernels, local(): pl.pallas_call(middle_kernel, out_shape=pltpu.VMEM((ROWS, CH), BF), in_sp...  8.66 us
    pallas_call x1, Pallas kernels, local(): pl.pallas_call(last_kernel, out_shape=[jax.ShapeDtypeStruct((COLS, CH), F...  7.35 us
    ppermute x1, starting transfers between devices, local(): north = lax.ppermute(lat_lo, 'ty', [(j, i) for i, j in line])  3.94 us
    ppermute x1, starting transfers between devices, local(): south = lax.ppermute(lat_hi, 'ty', line)  3.43 us
    ppermute x1, starting transfers between devices, local(): east = lax.ppermute(lon_lo, 'tx', [(j, i) for i, j in ring])  2.66 us
  transfers between devices with their start and end apart: 4, of which 0 were waited for; matrix products, arithmetic and copies ran while one was open for 0% of the time, Pallas kernels for 25%

commit v1 on v0

--- a/solution.py
+++ b/solution.py
@@ -17,6 +17,7 @@
 EDGE = 384
 EARLY = 6
 UNIT = 256
+EARLY_UNITS = 4
 BF, F32, I32 = jnp.bfloat16, jnp.float32, jnp.int32
 
 
@@ -94,6 +95,7 @@
     for c in w_copies:
         c.start()
     packed[...] = jnp.zeros_like(packed)
+    tend[...] = jnp.zeros_like(tend)
     st[0:LAT, :] = jnp.zeros((LAT, CH), F32)
     st[COLS + LAT : COLS + 2 * LAT, :] = jnp.zeros((LAT, CH), F32)
 
@@ -103,8 +105,6 @@
 
     mask_copy.wait()
     diff_copy.wait()
-    wait_quarter(0)
-    wait_quarter(1)
     dif_1 = dif[...].astype(BF).astype(F32)
     dif_2 = (dif[...] - dif_1).astype(BF).astype(F32)
     dif_3 = dif[...] - dif_1 - dif_2
@@ -167,7 +167,6 @@
         axis=1,
     )
     edge_n = jnp.broadcast_to(jnp.sum(edge_row, axis=1, keepdims=True), (1, LON))
-    stencil(0)
     scal_v[...] = jnp.where(iota((8, LON), 0) == 0, starts, edge_n).astype(I32)
     scal_copy = pltpu.make_async_copy(scal_v, scal, sem_s)
     scal_copy.start()
@@ -187,6 +186,9 @@
         for aligned, rows in todo:
             append(packed, rows, aligned)
 
+    wait_quarter(0)
+    stencil(0)
+    wait_quarter(1)
     scal_copy.wait()
 
     def both_steps(i, carry):
@@ -212,13 +214,7 @@
     before, _, _ = plan(scal)
     weights, hidden = (w_in, w_hid, w_out), (ha, hb)
 
-    @pl.when(before == 2)
-    def _():
-        tend[...] = closure_tile(packed[:TILE, :], *weights, *hidden)
-
-    @pl.when(before == 1)
-    def _():
-        tend[:UNIT, :] = closure_tile(packed[:UNIT, :], *weights, *hidden)
+    closure_units(packed, tend, weights, hidden, 0, before)
 
 
 def closure_units(packed, tend, weights, hidden, first, end):
@@ -243,24 +239,19 @@
     inner_n = scal[0, LON - 1]
     count = inner_n + scal[1, 0]
     total = lax.div(count + UNIT - 1, UNIT)
-    before = jnp.where(count >= 1536, 2, jnp.where(count >= 1280, 1, 0))
+    load = count + jnp.where(lax.axis_index("ty") == 0, TILE, 0)
     inner = lax.div(inner_n, UNIT)
+    most = jnp.where(lax.axis_index("ty") == 0, EARLY_UNITS, EARLY_UNITS - 2)
+    before = jnp.minimum(jnp.clip(lax.div(load, UNIT) - 4, 0, most), inner)
     less = (inner > before) & (lax.rem(inner - before, 2) == 1) & (total - inner < 2)
     return before, jnp.where(less, inner - 1, inner), total
 
 
 def middle_kernel(packed, tend_f, scal, w_in, w_hid, w_out, tend, ha, hb):
-    tend[...] = jnp.zeros_like(tend)
+    early = EARLY_UNITS * UNIT
+    tend[:early, :] = tend_f[...]
+    tend[early:, :] = jnp.zeros((ROWS - early, CH), BF)
     before, inner, _ = plan(scal)
-
-    @pl.when(before >= 1)
-    def _():
-        tend[:UNIT, :] = tend_f[:UNIT, :]
-
-    @pl.when(before == 2)
-    def _():
-        tend[UNIT:TILE, :] = tend_f[UNIT:, :]
-
     closure_units(packed, tend, (w_in, w_hid, w_out), (ha, hb), before, inner)
 
 
@@ -360,7 +351,7 @@
     kept = (
         ((COLS, CH), F32),
         ((ROWS, CH), BF),
-        ((TILE, CH), BF),
+        ((EARLY_UNITS * UNIT, CH), BF),
         ((LAT, LON), I32),
         ((8, EDGE), I32),
         None,

time: 35.3 us -> 33.1 us (0.938)
  the two profiles are of different devices: /device:TPU:5 before, /device:TPU:39 now
where the time goes in v1:
time: 33.1 us; the launch traced here: 32.9 us
  Pallas kernels  23.9 us (72%)
  starting transfers between devices  8.76 us (26%)
    pallas_call x1, Pallas kernels, local(): pl.pallas_call(middle_kernel, out_shape=pltpu.VMEM((ROWS, CH), BF), in_sp...  8.63 us
    pallas_call x1, Pallas kernels, local(): pl.pallas_call(first_kernel, out_shape=[pltpu.VMEM(*k) if k else pltpu.SM...  7.98 us
    pallas_call x1, Pallas kernels, local(): pl.pallas_call(last_kernel, out_shape=[jax.ShapeDtypeStruct((COLS, CH), F...  7.33 us
    ppermute x1, starting transfers between devices, local(): west = lax.ppermute(lon_hi, 'tx', ring)  3.19 us
    ppermute x1, starting transfers between devices, local(): north = lax.ppermute(lat_lo, 'ty', [(j, i) for i, j in line])  2.4 us
    ppermute x1, starting transfers between devices, local(): south = lax.ppermute(lat_hi, 'ty', line)  1.63 us
    ppermute x1, starting transfers between devices, local(): east = lax.ppermute(lon_lo, 'tx', [(j, i) for i, j in ring])  1.53 us
  transfers between devices with their start and end apart: 4, of which 0 were waited for; matrix products, arithmetic and copies ran while one was open for 0% of the time, Pallas kernels for 26%

profile of v1, /device:TPU:39, one launch (start us, length us, event | category | flops | bytes accessed | tf_op | source)
XLA Modules:
  0.0 32.9 jit_solution(10298098676871668539)
XLA Ops:
  0.0 8.0 %advance_pack.1 = (f32[4096,128]{1,0:T(8,128)S(1)}, bf16[2560,128]{1,0:T(8,128)(2,1)S(1)}, bf16[1024,128]{1,0:T(8,128)(2,1)S(1)}, s32[32,128]{1,0:T(8,128)S(1)},...) custom-call(f32[4096,128]{1,0:T(8,128)} %bitcast.5, ...), custom_call_target="tpu_custom_call" | custom-call | flops 1000000000 | bytes 1048576 | tf_op jit(solution)/shard_map/advance_pack/pallas_call | solution.py:368
  8.0 3.2 %collective-permute-start = (f32[32,128]{1,0:T(8,128)S(1)}, f32[32,128]{1,0:T(8,128)S(1)}, u32[]{:S(2)}, u32[]{:S(2)}) collective-permute-start(f32[32,128]{1,0:T(8,128)S(1)} %get-tuple-element.20), channel_id=1, source_target_pairs={{0,8},{8,16},{16,24},{24,0},{1,9},{9,17},{17,25},{25,1},{2,10},{10... | collective-permute-start | bytes 49160 | tf_op jit(solution)/shard_map/ppermute | solution.py:392
  11.2 1.5 %collective-permute-start.1 = (f32[32,128]{1,0:T(8,128)S(1)}, f32[32,128]{1,0:T(8,128)S(1)}, u32[]{:S(2)}, u32[]{:S(2)}) collective-permute-start(f32[32,128]{1,0:T(8,128)S(1)} %get-tuple-element.21), channel_id=1, source_target_pairs={{8,0},{16,8},{24,16},{0,24},{9,1},{17,9},{25,17},{1,25},{10,2},{18... | collective-permute-start | bytes 49160 | tf_op jit(solution)/shard_map/ppermute | solution.py:393
  12.7 1.6 %collective-permute-start.2 = (f32[128,128]{1,0:T(8,128)S(1)}, f32[128,128]{1,0:T(8,128)S(1)}, u32[]{:S(2)}, u32[]{:S(2)}) collective-permute-start(f32[128,128]{1,0:T(8,128)S(1)} %get-tuple-element.22), channel_id=1, source_target_pairs={{0,1},{1,2},{2,3},{3,4},{4,5},{5,6},{6,7},{7,0},{8,9},{9,10},{10,1... | collective-permute-start | bytes 196616 | tf_op jit(solution)/shard_map/ppermute | solution.py:394
  14.3 2.4 %collective-permute-start.3 = (f32[128,128]{1,0:T(8,128)S(1)}, f32[128,128]{1,0:T(8,128)S(1)}, u32[]{:S(2)}, u32[]{:S(2)}) collective-permute-start(f32[128,128]{1,0:T(8,128)S(1)} %get-tuple-element.23), channel_id=1, source_target_pairs={{1,0},{2,1},{3,2},{4,3},{5,4},{6,5},{7,6},{0,7},{9,8},{10,9},{11,1... | collective-permute-start | bytes 196616 | tf_op jit(solution)/shard_map/ppermute | solution.py:395
  16.7 8.6 %closure_middle.1.tend_i = bf16[2560,128]{1,0:T(8,128)(2,1)S(1)} custom-call(bf16[2560,128]{1,0:T(8,128)(2,1)S(1)} %get-tuple-element.25.packed.packed_i, bf16[1024,128]{1,0:T(8,128)(2,1)S(1)} %get-tuple-element.26.tend_f, s32[8,128]{1,0:T(8,128)S(4)} %get-tuple-element.27.scal, bf16[128,1024]{1,0:T(8,128)(2,1)S(1)} %get-tuple-element.28.w_in, ...), custom_call_target="tpu_custom_call" | custom-call | flops 12000000000 | bytes 1048576 | tf_op jit(solution)/shard_map/closure_middle/pallas_call | solution.py:396
  25.4 0.0 collective-permute-done.west
  25.4 0.0 collective-permute-done.1.east
  25.4 0.0 collective-permute-done.2.south
  25.4 0.0 collective-permute-done.3.north
  25.4 7.3 %closure_unpack.1 = (f32[4096,128]{1,0:T(8,128)}, f32[4096,128]{1,0:T(8,128)S(1)}, bf16[2560,128]{1,0:T(8,128)(2,1)S(1)}, bf16[2560,128]{1,0:T(8,128)(2,1)S(1)}) custom-call(f32[32,128]{1,0:T(8,128)S(1)} %collective-permute-done.west, f32[32,128]{1,0:T(8,128)S(1)} %collective-permute-done.1.east, ...), custom_call_target="tpu_custom_call", output_to_operand_aliasing={{1}: (4, {}), {2}: (5, {}), {3}: (6, {})} | custom-call | flops 4000000000 | bytes 1048576 | tf_op jit(solution)/shard_map/closure_unpack/pallas_call | solution.py:406
Async XLA Ops:
  8.0 17.4 %collective-permute-start = (f32[32,128]{1,0:T(8,128)S(1)}, f32[32,128]{1,0:T(8,128)S(1)}, u32[]{:S(2)}, u32[]{:S(2)}) collective-permute-start(f32[32,128]{1,0:T(8,128)S(1)} %get-tuple-element.20), channel_id=1, source_target_pairs={{0,8},{8,16},{16,24},{24,0},{1,9},{9,17},{17,25},{25,1},{2,10},{10... | collective-permute-start | bytes 49160 | tf_op jit(solution)/shard_map/ppermute | solution.py:392
  11.2 14.2 %collective-permute-start.1 = (f32[32,128]{1,0:T(8,128)S(1)}, f32[32,128]{1,0:T(8,128)S(1)}, u32[]{:S(2)}, u32[]{:S(2)}) collective-permute-start(f32[32,128]{1,0:T(8,128)S(1)} %get-tuple-element.21), channel_id=1, source_target_pairs={{8,0},{16,8},{24,16},{0,24},{9,1},{17,9},{25,17},{1,25},{10,2},{18... | collective-permute-start | bytes 49160 | tf_op jit(solution)/shard_map/ppermute | solution.py:393
  12.7 12.7 %collective-permute-start.2 = (f32[128,128]{1,0:T(8,128)S(1)}, f32[128,128]{1,0:T(8,128)S(1)}, u32[]{:S(2)}, u32[]{:S(2)}) collective-permute-start(f32[128,128]{1,0:T(8,128)S(1)} %get-tuple-element.22), channel_id=1, source_target_pairs={{0,1},{1,2},{2,3},{3,4},{4,5},{5,6},{6,7},{7,0},{8,9},{9,10},{10,1... | collective-permute-start | bytes 196616 | tf_op jit(solution)/shard_map/ppermute | solution.py:394
  14.3 11.1 %collective-permute-start.3 = (f32[128,128]{1,0:T(8,128)S(1)}, f32[128,128]{1,0:T(8,128)S(1)}, u32[]{:S(2)}, u32[]{:S(2)}) collective-permute-start(f32[128,128]{1,0:T(8,128)S(1)} %get-tuple-element.23), channel_id=1, source_target_pairs={{1,0},{2,1},{3,2},{4,3},{5,4},{6,5},{7,6},{0,7},{9,8},{10,9},{11,1... | collective-permute-start | bytes 196616 | tf_op jit(solution)/shard_map/ppermute | solution.py:395

commit v2 on v1

--- a/solution.py
+++ b/solution.py
@@ -239,10 +239,10 @@
     inner_n = scal[0, LON - 1]
     count = inner_n + scal[1, 0]
     total = lax.div(count + UNIT - 1, UNIT)
-    load = count + jnp.where(lax.axis_index("ty") == 0, TILE, 0)
+    place = lax.axis_index("ty")
+    more = jnp.where(place <= 1, 2, jnp.where(place <= 3, 1, 0))
     inner = lax.div(inner_n, UNIT)
-    most = jnp.where(lax.axis_index("ty") == 0, EARLY_UNITS, EARLY_UNITS - 2)
-    before = jnp.minimum(jnp.clip(lax.div(load, UNIT) - 4, 0, most), inner)
+    before = jnp.minimum(jnp.clip(lax.div(count, UNIT) - 4 + more, 0, EARLY_UNITS - 2 + more), inner)
     less = (inner > before) & (lax.rem(inner - before, 2) == 1) & (total - inner < 2)
     return before, jnp.where(less, inner - 1, inner), total
 

time: 33.1 us -> 33 us (level)
  the two profiles are of different devices: /device:TPU:39 before, /device:TPU:4 now
where the time goes in v2:
time: 33 us; the launch traced here: 32.7 us
  Pallas kernels  25.9 us (78%)
  starting transfers between devices  6.54 us (20%)
    pallas_call x1, Pallas kernels, local(): pl.pallas_call(first_kernel, out_shape=[pltpu.VMEM(*k) if k else pltpu.SM...  14 us
    pallas_call x1, Pallas kernels, local(): pl.pallas_call(last_kernel, out_shape=[jax.ShapeDtypeStruct((COLS, CH), F...  7.45 us
    pallas_call x1, Pallas kernels, local(): pl.pallas_call(middle_kernel, out_shape=pltpu.VMEM((ROWS, CH), BF), in_sp...  4.44 us
    ppermute x1, starting transfers between devices, local(): east = lax.ppermute(lon_lo, 'tx', [(j, i) for i, j in ring])  3.22 us
    ppermute x1, starting transfers between devices, local(): south = lax.ppermute(lat_hi, 'ty', line)  1.92 us
    ppermute x1, starting transfers between devices, local(): north = lax.ppermute(lat_lo, 'ty', [(j, i) for i, j in line])  1.31 us
  transfers between devices with their start and end apart: 4, of which 0 were waited for; matrix products, arithmetic and copies ran while one was open for 0% of the time, Pallas kernels for 14%

profile of v2, /device:TPU:4, one launch (start us, length us, event | category | flops | bytes accessed | tf_op | source)
XLA Modules:
  0.0 32.7 jit_solution(1189038835779621472)
XLA Ops:
  0.0 14.0 %advance_pack.1 = (f32[4096,128]{1,0:T(8,128)S(1)}, bf16[2560,128]{1,0:T(8,128)(2,1)S(1)}, bf16[1024,128]{1,0:T(8,128)(2,1)S(1)}, s32[32,128]{1,0:T(8,128)S(1)},...) custom-call(f32[4096,128]{1,0:T(8,128)} %bitcast.5, ...), custom_call_target="tpu_custom_call" | custom-call | flops 1000000000 | bytes 1048576 | tf_op jit(solution)/shard_map/advance_pack/pallas_call | solution.py:368
  14.0 0.1 collective-permute-start
  14.1 3.2 %collective-permute-start.1 = (f32[32,128]{1,0:T(8,128)S(1)}, f32[32,128]{1,0:T(8,128)S(1)}, u32[]{:S(2)}, u32[]{:S(2)}) collective-permute-start(f32[32,128]{1,0:T(8,128)S(1)} %get-tuple-element.21), channel_id=1, source_target_pairs={{8,0},{16,8},{24,16},{0,24},{9,1},{17,9},{25,17},{1,25},{10,2},{18... | collective-permute-start | bytes 49160 | tf_op jit(solution)/shard_map/ppermute | solution.py:393
  17.3 1.9 %collective-permute-start.2 = (f32[128,128]{1,0:T(8,128)S(1)}, f32[128,128]{1,0:T(8,128)S(1)}, u32[]{:S(2)}, u32[]{:S(2)}) collective-permute-start(f32[128,128]{1,0:T(8,128)S(1)} %get-tuple-element.22), channel_id=1, source_target_pairs={{0,1},{1,2},{2,3},{3,4},{4,5},{5,6},{6,7},{7,0},{8,9},{9,10},{10,1... | collective-permute-start | bytes 196616 | tf_op jit(solution)/shard_map/ppermute | solution.py:394
  19.2 1.3 %collective-permute-start.3 = (f32[128,128]{1,0:T(8,128)S(1)}, f32[128,128]{1,0:T(8,128)S(1)}, u32[]{:S(2)}, u32[]{:S(2)}) collective-permute-start(f32[128,128]{1,0:T(8,128)S(1)} %get-tuple-element.23), channel_id=1, source_target_pairs={{1,0},{2,1},{3,2},{4,3},{5,4},{6,5},{7,6},{0,7},{9,8},{10,9},{11,1... | collective-permute-start | bytes 196616 | tf_op jit(solution)/shard_map/ppermute | solution.py:395
  20.6 4.4 %closure_middle.1.tend_i = bf16[2560,128]{1,0:T(8,128)(2,1)S(1)} custom-call(bf16[2560,128]{1,0:T(8,128)(2,1)S(1)} %get-tuple-element.25.packed.packed_i, bf16[1024,128]{1,0:T(8,128)(2,1)S(1)} %get-tuple-element.26.tend_f, s32[8,128]{1,0:T(8,128)S(4)} %get-tuple-element.27.scal, bf16[128,1024]{1,0:T(8,128)(2,1)S(1)} %get-tuple-element.28.w_in, ...), custom_call_target="tpu_custom_call" | custom-call | flops 12000000000 | bytes 1048576 | tf_op jit(solution)/shard_map/closure_middle/pallas_call | solution.py:396
  25.0 0.0 collective-permute-done.west
  25.0 0.0 collective-permute-done.1.east
  25.0 0.0 collective-permute-done.2.south
  25.0 0.0 collective-permute-done.3.north
  25.0 7.4 %closure_unpack.1 = (f32[4096,128]{1,0:T(8,128)}, f32[4096,128]{1,0:T(8,128)S(1)}, bf16[2560,128]{1,0:T(8,128)(2,1)S(1)}, bf16[2560,128]{1,0:T(8,128)(2,1)S(1)}) custom-call(f32[32,128]{1,0:T(8,128)S(1)} %collective-permute-done.west, f32[32,128]{1,0:T(8,128)S(1)} %collective-permute-done.1.east, ...), custom_call_target="tpu_custom_call", output_to_operand_aliasing={{1}: (4, {}), {2}: (5, {}), {3}: (6, {})} | custom-call | flops 4000000000 | bytes 1048576 | tf_op jit(solution)/shard_map/closure_unpack/pallas_call | solution.py:406
Async XLA Ops:
  14.0 11.0 %collective-permute-start = (f32[32,128]{1,0:T(8,128)S(1)}, f32[32,128]{1,0:T(8,128)S(1)}, u32[]{:S(2)}, u32[]{:S(2)}) collective-permute-start(f32[32,128]{1,0:T(8,128)S(1)} %get-tuple-element.20), channel_id=1, source_target_pairs={{0,8},{8,16},{16,24},{24,0},{1,9},{9,17},{17,25},{25,1},{2,10},{10... | collective-permute-start | bytes 49160 | tf_op jit(solution)/shard_map/ppermute | solution.py:392
  14.1 10.9 %collective-permute-start.1 = (f32[32,128]{1,0:T(8,128)S(1)}, f32[32,128]{1,0:T(8,128)S(1)}, u32[]{:S(2)}, u32[]{:S(2)}) collective-permute-start(f32[32,128]{1,0:T(8,128)S(1)} %get-tuple-element.21), channel_id=1, source_target_pairs={{8,0},{16,8},{24,16},{0,24},{9,1},{17,9},{25,17},{1,25},{10,2},{18... | collective-permute-start | bytes 49160 | tf_op jit(solution)/shard_map/ppermute | solution.py:393
  17.3 7.7 %collective-permute-start.2 = (f32[128,128]{1,0:T(8,128)S(1)}, f32[128,128]{1,0:T(8,128)S(1)}, u32[]{:S(2)}, u32[]{:S(2)}) collective-permute-start(f32[128,128]{1,0:T(8,128)S(1)} %get-tuple-element.22), channel_id=1, source_target_pairs={{0,1},{1,2},{2,3},{3,4},{4,5},{5,6},{6,7},{7,0},{8,9},{9,10},{10,1... | collective-permute-start | bytes 196616 | tf_op jit(solution)/shard_map/ppermute | solution.py:394
  19.2 5.8 %collective-permute-start.3 = (f32[128,128]{1,0:T(8,128)S(1)}, f32[128,128]{1,0:T(8,128)S(1)}, u32[]{:S(2)}, u32[]{:S(2)}) collective-permute-start(f32[128,128]{1,0:T(8,128)S(1)} %get-tuple-element.23), channel_id=1, source_target_pairs={{1,0},{2,1},{3,2},{4,3},{5,4},{6,5},{7,6},{0,7},{9,8},{10,9},{11,1... | collective-permute-start | bytes 196616 | tf_op jit(solution)/shard_map/ppermute | solution.py:395

commit v3 on v2

--- a/solution.py
+++ b/solution.py
@@ -12,7 +12,7 @@
 TILE = 512
 CAP = 2048
 ROWS = CAP + TILE
-PGRP = 256
+PGRP = 128
 UGRP = 128
 EDGE = 384
 EARLY = 6
@@ -119,7 +119,7 @@
         spread = [jnp.where(own_lat, dif_n[pl.ds(i * 16 + j, 1), :], F32(0.0)) for j in range(16)]
         d_all = mm(jnp.concatenate(spread, axis=0).astype(BF), ones)
         for j in range(16):
-            r = pl.multiple_of(i * 2 * PGRP + j * LAT, LAT)
+            r = pl.multiple_of(i * 4 * PGRP + j * LAT, LAT)
             center = st[pl.ds(r + LAT, LAT), :]
             east = st[pl.ds(r + 2 * LAT, LAT), :]
             west = st[pl.ds(r, LAT), :]
@@ -178,9 +178,9 @@
     rank_e[...] = jnp.where(edge_row == 1.0, edge_rank + starts[:, LON - 1 :], F32(-4096.0)).astype(I32)
     def pack(i):
         todo = []
-        for k in range(2):
-            g = i * 2 + k
-            aligned = align16(scal[0, g * 8])
+        for k in range(4):
+            g = i * 4 + k
+            aligned = align16(scal[0, g * 4])
             hits = iota((PGRP + 16, PGRP), 0) == rank_r[pl.ds(g, 1), :] - aligned
             todo.append((aligned, mm(one_hot(hits), feat[pl.ds(pl.multiple_of(g * PGRP, PGRP), PGRP), :])))
         for aligned, rows in todo:

time: 33 us -> 32.6 us (0.988)
  the two profiles are of different devices: /device:TPU:4 before, /device:TPU:2 now
where the time goes in v3:
time: 32.6 us; the launch traced here: 32.5 us
  Pallas kernels  25.7 us (79%)
  starting transfers between devices  6.54 us (20%)
    pallas_call x1, Pallas kernels, local(): pl.pallas_call(first_kernel, out_shape=[pltpu.VMEM(*k) if k else pltpu.SM...  13.9 us
    pallas_call x1, Pallas kernels, local(): pl.pallas_call(last_kernel, out_shape=[jax.ShapeDtypeStruct((COLS, CH), F...  7.45 us
    pallas_call x1, Pallas kernels, local(): pl.pallas_call(middle_kernel, out_shape=pltpu.VMEM((ROWS, CH), BF), in_sp...  4.44 us
    ppermute x1, starting transfers between devices, local(): east = lax.ppermute(lon_lo, 'tx', [(j, i) for i, j in ring])  3.22 us
    ppermute x1, starting transfers between devices, local(): south = lax.ppermute(lat_hi, 'ty', line)  1.91 us
    ppermute x1, starting transfers between devices, local(): north = lax.ppermute(lat_lo, 'ty', [(j, i) for i, j in line])  1.32 us
  transfers between devices with their start and end apart: 4, of which 0 were waited for; matrix products, arithmetic and copies ran while one was open for 0% of the time, Pallas kernels for 14%

profile of v3, /device:TPU:2, one launch (start us, length us, event | category | flops | bytes accessed | tf_op | source)
XLA Modules:
  0.0 32.5 jit_solution(3653868689146986635)
XLA Ops:
  0.0 13.9 %advance_pack.1 = (f32[4096,128]{1,0:T(8,128)S(1)}, bf16[2560,128]{1,0:T(8,128)(2,1)S(1)}, bf16[1024,128]{1,0:T(8,128)(2,1)S(1)}, s32[32,128]{1,0:T(8,128)S(1)},...) custom-call(f32[4096,128]{1,0:T(8,128)} %bitcast.5, ...), custom_call_target="tpu_custom_call" | custom-call | flops 1000000000 | bytes 1048576 | tf_op jit(solution)/shard_map/advance_pack/pallas_call | solution.py:368
  13.9 0.1 collective-permute-start
  14.0 3.2 %collective-permute-start.1 = (f32[32,128]{1,0:T(8,128)S(1)}, f32[32,128]{1,0:T(8,128)S(1)}, u32[]{:S(2)}, u32[]{:S(2)}) collective-permute-start(f32[32,128]{1,0:T(8,128)S(1)} %get-tuple-element.21), channel_id=1, source_target_pairs={{8,0},{16,8},{24,16},{0,24},{9,1},{17,9},{25,17},{1,25},{10,2},{18... | collective-permute-start | bytes 49160 | tf_op jit(solution)/shard_map/ppermute | solution.py:393
  17.2 1.9 %collective-permute-start.2 = (f32[128,128]{1,0:T(8,128)S(1)}, f32[128,128]{1,0:T(8,128)S(1)}, u32[]{:S(2)}, u32[]{:S(2)}) collective-permute-start(f32[128,128]{1,0:T(8,128)S(1)} %get-tuple-element.22), channel_id=1, source_target_pairs={{0,1},{1,2},{2,3},{3,4},{4,5},{5,6},{6,7},{7,0},{8,9},{9,10},{10,1... | collective-permute-start | bytes 196616 | tf_op jit(solution)/shard_map/ppermute | solution.py:394
  19.1 1.3 %collective-permute-start.3 = (f32[128,128]{1,0:T(8,128)S(1)}, f32[128,128]{1,0:T(8,128)S(1)}, u32[]{:S(2)}, u32[]{:S(2)}) collective-permute-start(f32[128,128]{1,0:T(8,128)S(1)} %get-tuple-element.23), channel_id=1, source_target_pairs={{1,0},{2,1},{3,2},{4,3},{5,4},{6,5},{7,6},{0,7},{9,8},{10,9},{11,1... | collective-permute-start | bytes 196616 | tf_op jit(solution)/shard_map/ppermute | solution.py:395
  20.4 4.4 %closure_middle.1.tend_i = bf16[2560,128]{1,0:T(8,128)(2,1)S(1)} custom-call(bf16[2560,128]{1,0:T(8,128)(2,1)S(1)} %get-tuple-element.25.packed.packed_i, bf16[1024,128]{1,0:T(8,128)(2,1)S(1)} %get-tuple-element.26.tend_f, s32[8,128]{1,0:T(8,128)S(4)} %get-tuple-element.27.scal, bf16[128,1024]{1,0:T(8,128)(2,1)S(1)} %get-tuple-element.28.w_in, ...), custom_call_target="tpu_custom_call" | custom-call | flops 12000000000 | bytes 1048576 | tf_op jit(solution)/shard_map/closure_middle/pallas_call | solution.py:396
  24.9 0.0 collective-permute-done.west
  24.9 0.0 collective-permute-done.1.east
  24.9 0.0 collective-permute-done.2.south
  24.9 0.0 collective-permute-done.3.north
  24.9 7.4 %closure_unpack.1 = (f32[4096,128]{1,0:T(8,128)}, f32[4096,128]{1,0:T(8,128)S(1)}, bf16[2560,128]{1,0:T(8,128)(2,1)S(1)}, bf16[2560,128]{1,0:T(8,128)(2,1)S(1)}) custom-call(f32[32,128]{1,0:T(8,128)S(1)} %collective-permute-done.west, f32[32,128]{1,0:T(8,128)S(1)} %collective-permute-done.1.east, ...), custom_call_target="tpu_custom_call", output_to_operand_aliasing={{1}: (4, {}), {2}: (5, {}), {3}: (6, {})} | custom-call | flops 4000000000 | bytes 1048576 | tf_op jit(solution)/shard_map/closure_unpack/pallas_call | solution.py:406
Async XLA Ops:
  13.9 11.0 %collective-permute-start = (f32[32,128]{1,0:T(8,128)S(1)}, f32[32,128]{1,0:T(8,128)S(1)}, u32[]{:S(2)}, u32[]{:S(2)}) collective-permute-start(f32[32,128]{1,0:T(8,128)S(1)} %get-tuple-element.20), channel_id=1, source_target_pairs={{0,8},{8,16},{16,24},{24,0},{1,9},{9,17},{17,25},{25,1},{2,10},{10... | collective-permute-start | bytes 49160 | tf_op jit(solution)/shard_map/ppermute | solution.py:392
  14.0 10.9 %collective-permute-start.1 = (f32[32,128]{1,0:T(8,128)S(1)}, f32[32,128]{1,0:T(8,128)S(1)}, u32[]{:S(2)}, u32[]{:S(2)}) collective-permute-start(f32[32,128]{1,0:T(8,128)S(1)} %get-tuple-element.21), channel_id=1, source_target_pairs={{8,0},{16,8},{24,16},{0,24},{9,1},{17,9},{25,17},{1,25},{10,2},{18... | collective-permute-start | bytes 49160 | tf_op jit(solution)/shard_map/ppermute | solution.py:393
  17.2 7.7 %collective-permute-start.2 = (f32[128,128]{1,0:T(8,128)S(1)}, f32[128,128]{1,0:T(8,128)S(1)}, u32[]{:S(2)}, u32[]{:S(2)}) collective-permute-start(f32[128,128]{1,0:T(8,128)S(1)} %get-tuple-element.22), channel_id=1, source_target_pairs={{0,1},{1,2},{2,3},{3,4},{4,5},{5,6},{6,7},{7,0},{8,9},{9,10},{10,1... | collective-permute-start | bytes 196616 | tf_op jit(solution)/shard_map/ppermute | solution.py:394
  19.1 5.8 %collective-permute-start.3 = (f32[128,128]{1,0:T(8,128)S(1)}, f32[128,128]{1,0:T(8,128)S(1)}, u32[]{:S(2)}, u32[]{:S(2)}) collective-permute-start(f32[128,128]{1,0:T(8,128)S(1)} %get-tuple-element.23), channel_id=1, source_target_pairs={{1,0},{2,1},{3,2},{4,3},{5,4},{6,5},{7,6},{0,7},{9,8},{10,9},{11,1... | collective-permute-start | bytes 196616 | tf_op jit(solution)/shard_map/ppermute | solution.py:395

commit v4 on v3

--- a/solution.py
+++ b/solution.py
@@ -287,15 +287,26 @@
         adv[pl.ds(r, 4 * UGRP), :] += jnp.concatenate(parts, axis=0)
 
     _, done, total = plan(scal)
-    early = (total - done >= 2) & (scal[0, EARLY * 16] <= (total - 2) * UNIT)
+    ready = scal[0, EARLY * 16]
+    early_tile = (total - done >= 2) & (ready <= (total - 2) * UNIT)
+    early_unit = (total - done == 1) & (ready <= (total - 1) * UNIT)
+    early = early_tile | early_unit
     weights, hidden = (w_in, w_hid, w_out), (ha, hb)
-    closure_units(packed, tend, weights, hidden, done, jnp.where(early, total - 2, total))
-
-    @pl.when(early)
-    def _():
-        part = pl.ds(pl.multiple_of((total - 2) * UNIT, UNIT), TILE)
+    plain = jnp.where(early_tile, total - 2, jnp.where(early_unit, total - 1, total))
+    closure_units(packed, tend, weights, hidden, done, plain)
+
+    def last_rows(first, size):
+        part = pl.ds(pl.multiple_of(first * UNIT, UNIT), size)
         beside = [functools.partial(unpacked, q) for q in range(EARLY)]
         tend[part, :] = closure_tile(packed[part, :], *weights, *hidden, beside)
+
+    @pl.when(early_tile)
+    def _():
+        last_rows(total - 2, TILE)
+
+    @pl.when(early_unit)
+    def _():
+        last_rows(total - 1, UNIT)
 
     rank_col = jnp.concatenate(
         [jnp.transpose(jnp.broadcast_to(rank_e[:1, k * 128 : k * 128 + 128], (128, 128))) for k in range(3)], axis=0

time: 32.6 us -> 32.4 us (level)
  the two profiles are of different devices: /device:TPU:2 before, /device:TPU:96 now
where the time goes in v4:
time: 32.4 us; the launch traced here: 31.9 us
  Pallas kernels  26.3 us (81%)
  starting transfers between devices  5.33 us (16%)
    pallas_call x1, Pallas kernels, local(): pl.pallas_call(first_kernel, out_shape=[pltpu.VMEM(*k) if k else pltpu.SM...  12 us
    pallas_call x1, Pallas kernels, local(): pl.pallas_call(last_kernel, out_shape=[jax.ShapeDtypeStruct((COLS, CH), F...  7.45 us
    pallas_call x1, Pallas kernels, local(): pl.pallas_call(middle_kernel, out_shape=pltpu.VMEM((ROWS, CH), BF), in_sp...  6.84 us
    ppermute x1, starting transfers between devices, local(): east = lax.ppermute(lon_lo, 'tx', [(j, i) for i, j in ring])  3.22 us
    ppermute x1, starting transfers between devices, local(): north = lax.ppermute(lat_lo, 'ty', [(j, i) for i, j in line])  1.42 us
  transfers between devices with their start and end apart: 4, of which 0 were waited for; matrix products, arithmetic and copies ran while one was open for 0% of the time, Pallas kernels for 21%

profile of v4, /device:TPU:96, one launch (start us, length us, event | category | flops | bytes accessed | tf_op | source)
XLA Modules:
  0.0 31.9 jit_solution(2831777116907566222)
XLA Ops:
  0.0 12.0 %advance_pack.1 = (f32[4096,128]{1,0:T(8,128)S(1)}, bf16[2560,128]{1,0:T(8,128)(2,1)S(1)}, bf16[1024,128]{1,0:T(8,128)(2,1)S(1)}, s32[32,128]{1,0:T(8,128)S(1)},...) custom-call(f32[4096,128]{1,0:T(8,128)} %bitcast.5, ...), custom_call_target="tpu_custom_call" | custom-call | flops 1000000000 | bytes 1048576 | tf_op jit(solution)/shard_map/advance_pack/pallas_call | solution.py:379
  12.1 0.1 collective-permute-start
  12.1 3.2 %collective-permute-start.1 = (f32[32,128]{1,0:T(8,128)S(1)}, f32[32,128]{1,0:T(8,128)S(1)}, u32[]{:S(2)}, u32[]{:S(2)}) collective-permute-start(f32[32,128]{1,0:T(8,128)S(1)} %get-tuple-element.21), channel_id=1, source_target_pairs={{8,0},{16,8},{24,16},{0,24},{9,1},{17,9},{25,17},{1,25},{10,2},{18... | collective-permute-start | bytes 49160 | tf_op jit(solution)/shard_map/ppermute | solution.py:404
  15.4 0.6 %collective-permute-start.2 = (f32[128,128]{1,0:T(8,128)S(1)}, f32[128,128]{1,0:T(8,128)S(1)}, u32[]{:S(2)}, u32[]{:S(2)}) collective-permute-start(f32[128,128]{1,0:T(8,128)S(1)} %get-tuple-element.22), channel_id=1, source_target_pairs={{0,1},{1,2},{2,3},{3,4},{4,5},{5,6},{6,7},{7,0},{8,9},{9,10},{10,1... | collective-permute-start | bytes 196616 | tf_op jit(solution)/shard_map/ppermute | solution.py:405
  16.0 1.4 %collective-permute-start.3 = (f32[128,128]{1,0:T(8,128)S(1)}, f32[128,128]{1,0:T(8,128)S(1)}, u32[]{:S(2)}, u32[]{:S(2)}) collective-permute-start(f32[128,128]{1,0:T(8,128)S(1)} %get-tuple-element.23), channel_id=1, source_target_pairs={{1,0},{2,1},{3,2},{4,3},{5,4},{6,5},{7,6},{0,7},{9,8},{10,9},{11,1... | collective-permute-start | bytes 196616 | tf_op jit(solution)/shard_map/ppermute | solution.py:406
  17.4 6.8 %closure_middle.1.tend_i = bf16[2560,128]{1,0:T(8,128)(2,1)S(1)} custom-call(bf16[2560,128]{1,0:T(8,128)(2,1)S(1)} %get-tuple-element.25.packed.packed_i, bf16[1024,128]{1,0:T(8,128)(2,1)S(1)} %get-tuple-element.26.tend_f, s32[8,128]{1,0:T(8,128)S(4)} %get-tuple-element.27.scal, bf16[128,1024]{1,0:T(8,128)(2,1)S(1)} %get-tuple-element.28.w_in, ...), custom_call_target="tpu_custom_call" | custom-call | flops 12000000000 | bytes 1048576 | tf_op jit(solution)/shard_map/closure_middle/pallas_call | solution.py:407
  24.2 0.0 collective-permute-done.west
  24.3 0.0 collective-permute-done.1.east
  24.3 0.0 collective-permute-done.2.south
  24.3 0.0 collective-permute-done.3.north
  24.3 7.5 %closure_unpack.1 = (f32[4096,128]{1,0:T(8,128)}, f32[4096,128]{1,0:T(8,128)S(1)}, bf16[2560,128]{1,0:T(8,128)(2,1)S(1)}, bf16[2560,128]{1,0:T(8,128)(2,1)S(1)}) custom-call(f32[32,128]{1,0:T(8,128)S(1)} %collective-permute-done.west, f32[32,128]{1,0:T(8,128)S(1)} %collective-permute-done.1.east, ...), custom_call_target="tpu_custom_call", output_to_operand_aliasing={{1}: (4, {}), {2}: (5, {}), {3}: (6, {})} | custom-call | flops 4000000000 | bytes 1048576 | tf_op jit(solution)/shard_map/closure_unpack/pallas_call | solution.py:417
Async XLA Ops:
  12.1 12.2 %collective-permute-start = (f32[32,128]{1,0:T(8,128)S(1)}, f32[32,128]{1,0:T(8,128)S(1)}, u32[]{:S(2)}, u32[]{:S(2)}) collective-permute-start(f32[32,128]{1,0:T(8,128)S(1)} %get-tuple-element.20), channel_id=1, source_target_pairs={{0,8},{8,16},{16,24},{24,0},{1,9},{9,17},{17,25},{25,1},{2,10},{10... | collective-permute-start | bytes 49160 | tf_op jit(solution)/shard_map/ppermute | solution.py:403
  12.1 12.1 %collective-permute-start.1 = (f32[32,128]{1,0:T(8,128)S(1)}, f32[32,128]{1,0:T(8,128)S(1)}, u32[]{:S(2)}, u32[]{:S(2)}) collective-permute-start(f32[32,128]{1,0:T(8,128)S(1)} %get-tuple-element.21), channel_id=1, source_target_pairs={{8,0},{16,8},{24,16},{0,24},{9,1},{17,9},{25,17},{1,25},{10,2},{18... | collective-permute-start | bytes 49160 | tf_op jit(solution)/shard_map/ppermute | solution.py:404
  15.4 8.9 %collective-permute-start.2 = (f32[128,128]{1,0:T(8,128)S(1)}, f32[128,128]{1,0:T(8,128)S(1)}, u32[]{:S(2)}, u32[]{:S(2)}) collective-permute-start(f32[128,128]{1,0:T(8,128)S(1)} %get-tuple-element.22), channel_id=1, source_target_pairs={{0,1},{1,2},{2,3},{3,4},{4,5},{5,6},{6,7},{7,0},{8,9},{9,10},{10,1... | collective-permute-start | bytes 196616 | tf_op jit(solution)/shard_map/ppermute | solution.py:405
  16.0 8.3 %collective-permute-start.3 = (f32[128,128]{1,0:T(8,128)S(1)}, f32[128,128]{1,0:T(8,128)S(1)}, u32[]{:S(2)}, u32[]{:S(2)}) collective-permute-start(f32[128,128]{1,0:T(8,128)S(1)} %get-tuple-element.23), channel_id=1, source_target_pairs={{1,0},{2,1},{3,2},{4,3},{5,4},{6,5},{7,6},{0,7},{9,8},{10,9},{11,1... | collective-permute-start | bytes 196616 | tf_op jit(solution)/shard_map/ppermute | solution.py:406
